TPU v7x, 128 devices: a whole 4x4x4 slice. The times are simulated.
128 devices in a mesh: ent: 128 (over z, y, x, core).
Axes of the slice: x: 4, y: 4, z: 4, core: 2. Of those that a mesh axis runs over, the one named last changes fastest.
Arguments:
- mentions: bfloat16 [131072, 768], P('ent'), may hold values from -6 to 6
- table: bfloat16 [524288, 768], P('ent'), may hold values from -2 to 2
- picks: int32 [128, 8], P('ent'), may hold values from 0 to 15
- gold: int32 [131072], P('ent'), may hold values from 0 to 2047
Outputs:
- loss: float32 [], replicated
- d_mentions: float32 [131072, 768], P('ent')
- d_table: float32 [524288, 768], P('ent')
All inputs are finite; a program needn't handle non-finite values.
Results may differ from a plain program's by a relative error of at most 0.002.
Values may be sent and summed in bfloat16 or wider, within the bound.
A program may use at most 128 MiB of HBM per device.

v0:
```python
import functools

import jax
import jax.numpy as jnp
from jax import lax
from jax.sharding import Mesh
from jax.sharding import PartitionSpec as P

BLK = 256
ROUNDS = 8
MEN = 1024
ENT = ("ent_0", "ent_1", "ent_2", "ent_3")


def from_behind(value, axis, by):
    length = lax.axis_size(axis)
    return lax.ppermute(value, axis, [(i, (i + by) % length) for i in range(length)])


def over_axes(value, axes):
    return functools.reduce(lax.psum, axes, value)


def on_device(mentions, table, picks, gold):
    count = lax.axis_size(ENT)
    stride = count // ROUNDS
    width = table.shape[1]
    local = table.reshape(-1, BLK, width)
    nblocks = local.shape[0]
    served = jnp.take(local, picks[0], axis=0)
    pieces = [from_behind(served[j], ENT, j * stride + 1) for j in range(ROUNDS)]
    cand = jnp.concatenate(pieces, axis=0)
    scores = lax.dot_general(
        mentions, cand, (((1,), (1,)), ((), ())), preferred_element_type=jnp.float32
    )
    top = jnp.max(scores, axis=1, keepdims=True)
    lse = top[:, 0] + jnp.log(jnp.sum(jnp.exp(scores - top), axis=1))
    target = jnp.take_along_axis(scores, gold[:, None], axis=1)[:, 0]
    partial_loss = jnp.sum(lse - target)
    onehot = (jnp.arange(cand.shape[0], dtype=jnp.int32)[None, :] == gold[:, None]).astype(
        jnp.float32
    )
    dscore = (jnp.exp(scores - lse[:, None]) - onehot).astype(jnp.bfloat16)
    d_mentions = jnp.dot(dscore, cand, preferred_element_type=jnp.float32)
    dcand = lax.dot_general(
        dscore, mentions, (((0,), (0,)), ((), ())), preferred_element_type=jnp.float32
    )
    dblocks = dcand.reshape(ROUNDS, BLK, width)
    returned = jnp.stack([from_behind(dblocks[j], ENT, -(j * stride + 1)) for j in range(ROUNDS)])
    selector = (picks[0][:, None] == jnp.arange(nblocks, dtype=jnp.int32)[None, :]).astype(
        jnp.float32
    )
    d_table = jnp.einsum(
        "jb,jrd->brd", selector, returned, precision=lax.Precision.HIGHEST
    ).reshape(-1, width)
    total = over_axes(partial_loss, ENT)
    loss = total / jnp.float32(count * MEN)
    return (loss, d_mentions, d_table)


def solution(mesh):
    finer = Mesh(mesh.devices.reshape(4, 4, 4, 2), ("ent_0", "ent_1", "ent_2", "ent_3"))
    in_specs = (P(ENT, None), P(ENT, None), P(ENT, None), P(ENT))
    out_specs = (P(), P(ENT, None), P(ENT, None))
    return jax.shard_map(
        on_device, mesh=finer, in_specs=in_specs, out_specs=out_specs, check_vma=False
    )
```

profile of v0, /device:TPU:24, one launch (start us, length us, event | category | flops | bytes accessed | tf_op | source)
XLA Modules:
  0.0 274.3 jit_solution(13761731164751403172)
XLA Ops:
  0.6 0.0 copy-start
  0.6 0.8 compare_and_fusion
  1.4 0.7 fusion.10
  2.1 5.2 %gather_fusion = bf16[8,256,768]{2,1,0:T(8,128)(2,1)} fusion(bf16[16,256,768]{2,1,0:T(8,128)(2,1)} %bitcast.64, s32[1024]{0:T(1024)S(1)} %pad_clamp_fusion), kind=kCustom, calls=%fused_computation | custom fusion | bytes 6291488 | tf_op jit(solution)/shard_map/jit(_take)/gather | solution.py:30
  7.3 2.3 broadcast_select_fusion
  9.6 0.2 slice_bitcast_fusion
  9.8 0.7 collective-permute-start.7
  10.5 6.4 %collective-permute-start.3 = (bf16[256,768]{1,0:T(8,128)(2,1)S(1)}, bf16[256,768]{1,0:T(8,128)(2,1)S(1)}, u32[]{:S(2)}, u32[]{:S(2)}) collective-permute-start(bf16[256,768]{1,0:T(8,128)(2,1)S(1)} %get-tuple-element.17), channel_id=1, source_target_pairs={{0,49},{1,50},{2,51},{3,52},{4,53},{5,54},{6,55},{7,56},{8,57},{9,... | collective-permute-start | bytes 1179656 | tf_op jit(solution)/shard_map/ppermute | solution.py:17
  16.9 0.8 collective-permute-start.2
  17.6 2.6 collective-permute-start.1
  20.2 0.0 collective-permute-start
  20.3 17.6 %collective-permute-done = bf16[256,768]{1,0:T(8,128)(2,1)S(1)} collective-permute-done((bf16[256,768]{1,0:T(8,128)(2,1)S(1)}, bf16[256,768]{1,0:T(8,128)(2,1)S(1)}, u32[]{:S(2)}, u32[]{:S(2)}) %collective-permute-start) | collective-permute-done | bytes 393248 | tf_op jit(solution)/shard_map/ppermute | solution.py:17
  37.9 1.6 collective-permute-start.4
  39.5 5.2 %collective-permute-done.1 = bf16[256,768]{1,0:T(8,128)(2,1)S(1)} collective-permute-done((bf16[256,768]{1,0:T(8,128)(2,1)S(1)}, bf16[256,768]{1,0:T(8,128)(2,1)S(1)}, u32[]{:S(2)}, u32[]{:S(2)}) %collective-permute-start.1) | collective-permute-done | bytes 393248 | tf_op jit(solution)/shard_map/ppermute | solution.py:17
  44.7 2.3 collective-permute-start.5
  47.0 0.0 collective-permute-done.2
  47.0 0.1 collective-permute-start.6
  47.1 0.0 collective-permute-done.3
  47.2 2.5 collective-permute-done.4
  49.8 13.6 %collective-permute-done.5 = bf16[256,768]{1,0:T(8,128)(2,1)S(1)} collective-permute-done((bf16[256,768]{1,0:T(8,128)(2,1)S(1)}, bf16[256,768]{1,0:T(8,128)(2,1)S(1)}, u32[]{:S(2)}, u32[]{:S(2)}) %collective-permute-start.5) | collective-permute-done | bytes 393248 | tf_op jit(solution)/shard_map/ppermute | solution.py:17
  63.4 5.8 %collective-permute-done.6 = bf16[256,768]{1,0:T(8,128)(2,1)S(1)} collective-permute-done((bf16[256,768]{1,0:T(8,128)(2,1)S(1)}, bf16[256,768]{1,0:T(8,128)(2,1)S(1)}, u32[]{:S(2)}, u32[]{:S(2)}) %collective-permute-start.6) | collective-permute-done | bytes 393248 | tf_op jit(solution)/shard_map/ppermute | solution.py:17
  69.3 0.0 collective-permute-done.7
  69.3 0.0 copy-start.4
  69.4 3.6 %fusion.14 = (f32[1024]{0:T(1024)S(1)}, f32[2048,1024]{1,0:T(8,128)S(1)}) fusion(bf16[2048,768]{1,0:T(8,128)(2,1)S(1)} %constant_dynamic-update-slice_fusion, bf16[1024,768]{1,0:T(8,128)(2,1)S(1)} %copy-done), kind=kOutput, calls=%fused_computation.54 | convolution fusion | flops 3223321600 | bytes 13111296 | tf_op jit(solution)/shard_map/dot_general | solution.py:33
  73.0 0.0 copy-start.2
  73.0 3.4 %copy-done.2 = f32[2048,1024]{1,0:T(8,128)} copy-done((f32[2048,1024]{1,0:T(8,128)}, f32[2048,1024]{1,0:T(8,128)S(1)}, u32[]{:S(2)}) %copy-start.2) | copy-done | bytes 8388632
  76.4 1.2 exponential_reduce_fusion
  77.6 13.7 %gather_fusion.1 = f32[1024]{0:T(1024)S(1)} fusion(f32[1024,2048]{0,1:T(8,128)} %bitcast.62, s32[1024]{0:T(1024)S(1)} %bitcast.61), kind=kCustom, calls=%fused_computation.1 | custom fusion | bytes 16384 | tf_op jit(solution)/shard_map/jit(take_along_axis)/gather | solution.py:38
  91.2 0.6 subtract_reduce_fusion
  91.9 10.8 %psum.28 = f32[]{:T(128)} all-reduce(f32[]{:T(128)} %get-tuple-element.3), channel_id=1, replica_groups=mesh['ent_0'=4,'ent_1'=4,'ent_2'=4,'ent_3'=2] {'ent_0'}, use_global_device_ids=true, to_apply=%region_3.4 | all-reduce | flops 1 | bytes 8 | tf_op jit(solution)/shard_map/psum | solution.py:21
  102.6 10.2 %psum.29 = f32[]{:T(128)} all-reduce(f32[]{:T(128)} %psum.28), channel_id=1, replica_groups=mesh['ent_0'=4,'ent_1'=4,'ent_2'=4,'ent_3'=2] {'ent_1'}, use_global_device_ids=true, to_apply=%region_4.5 | all-reduce | flops 1 | bytes 8 | tf_op jit(solution)/shard_map/psum | solution.py:21
  112.9 8.3 %psum.30 = f32[]{:T(128)} all-reduce(f32[]{:T(128)} %psum.29), channel_id=1, replica_groups=mesh['ent_0'=4,'ent_1'=4,'ent_2'=4,'ent_3'=2] {'ent_2'}, use_global_device_ids=true, to_apply=%region_5.6 | all-reduce | flops 1 | bytes 8 | tf_op jit(solution)/shard_map/psum | solution.py:21
  121.2 6.7 %fusion.2 = f32[2048,768]{1,0:T(8,128)S(1)} fusion(bf16[1024,768]{1,0:T(8,128)(2,1)S(1)} %copy-done, s32[1024]{0:T(1024)S(1)} %copy-done.6, f32[1024]{0:T(1024)S(1)} %get-tuple-element.4, f32[2048,1024]{1,0:T(8,128)} %copy-done.2), kind=kOutput, calls=%fused_computation.24 | convolution fusion | flops 3231711232 | bytes 16261120 | tf_op jit(solution)/shard_map/dot_general | solution.py:45
  127.9 0.0 copy-start.3
  127.9 0.0 copy-start.5
  128.0 2.0 fusion.13
  129.9 0.0 collective-permute-start.10
  129.9 3.7 %collective-permute-start.9 = (f32[256,768]{1,0:T(8,128)}, f32[256,768]{1,0:T(8,128)}, u32[]{:S(2)}, u32[]{:S(2)}) collective-permute-start(f32[256,768]{1,0:T(8,128)} %get-tuple-element.11), channel_id=1, source_target_pairs={{0,111},{1,112},{2,113},{3,114},{4,115},{5,116},{6,117},{7,118},{8... | collective-permute-start | bytes 2359304 | tf_op jit(solution)/shard_map/ppermute | solution.py:17
  133.6 0.0 collective-permute-start.8
  133.6 5.8 %fusion.3 = f32[1024,768]{1,0:T(8,128)} fusion(bf16[2048,768]{1,0:T(8,128)(2,1)S(1)} %copy-done.5, s32[1024]{0:T(1024)S(1)} %copy-done.6, f32[1024]{0:T(1024)S(1)} %get-tuple-element.4, f32[2048,1024]{1,0:T(8,128)S(1)} %copy-done.3), kind=kOutput, calls=%fused_computation.25 | convolution fusion | flops 3231711232 | bytes 14688256 | tf_op jit(solution)/shard_map/dot_general | solution.py:44
  139.4 3.2 %psum.31 = f32[]{:T(128)} all-reduce(f32[]{:T(128)} %psum.30), channel_id=1, replica_groups=mesh['ent_0'=4,'ent_1'=4,'ent_2'=4,'ent_3'=2] {'ent_3'}, use_global_device_ids=true, to_apply=%region_6.7 | all-reduce | flops 1 | bytes 8 | tf_op jit(solution)/shard_map/psum | solution.py:21
  142.7 2.7 collective-permute-start.15
  145.4 0.0 collective-permute-start.14
  146.0 18.3 %collective-permute-done.8 = f32[256,768]{1,0:T(8,128)} collective-permute-done((f32[256,768]{1,0:T(8,128)}, f32[256,768]{1,0:T(8,128)}, u32[]{:S(2)}, u32[]{:S(2)}) %collective-permute-start.8) | collective-permute-done | bytes 786464 | tf_op jit(solution)/shard_map/ppermute | solution.py:17
  164.3 5.2 %collective-permute-start.11 = (f32[256,768]{1,0:T(8,128)}, f32[256,768]{1,0:T(8,128)S(1)}, u32[]{:S(2)}, u32[]{:S(2)}) collective-permute-start(f32[256,768]{1,0:T(8,128)} %get-tuple-element.9), channel_id=1, source_target_pairs={{0,79},{1,80},{2,81},{3,82},{4,83},{5,84},{6,85},{7,86},{8,87},{9,... | collective-permute-start | bytes 2359304 | tf_op jit(solution)/shard_map/ppermute | solution.py:17
  169.5 1.2 bitcast_dynamic-update-slice_fusion.7
  170.7 0.0 collective-permute-done.9
  170.7 0.1 collective-permute-start.12
  170.8 1.2 bitcast_dynamic-update-slice_fusion.6
  171.9 0.0 collective-permute-done.10
  172.0 2.8 %collective-permute-start.13 = (f32[256,768]{1,0:T(8,128)S(1)}, f32[256,768]{1,0:T(8,128)S(1)}, u32[]{:S(2)}, u32[]{:S(2)}) collective-permute-start(f32[256,768]{1,0:T(8,128)S(1)} %get-tuple-element.7), channel_id=1, source_target_pairs={{0,47},{1,48},{2,49},{3,50},{4,51},{5,52},{6,53},{7,54},{8,55},{9,... | collective-permute-start | bytes 2359304 | tf_op jit(solution)/shard_map/ppermute | solution.py:17
  174.7 1.2 bitcast_dynamic-update-slice_fusion.5
  175.9 34.4 %collective-permute-done.11 = f32[256,768]{1,0:T(8,128)S(1)} collective-permute-done((f32[256,768]{1,0:T(8,128)}, f32[256,768]{1,0:T(8,128)S(1)}, u32[]{:S(2)}, u32[]{:S(2)}) %collective-permute-start.11) | collective-permute-done | bytes 786464 | tf_op jit(solution)/shard_map/ppermute | solution.py:17
  210.3 0.1 bitcast_dynamic-update-slice_fusion.4
  210.4 33.9 %collective-permute-done.12 = f32[256,768]{1,0:T(8,128)S(1)} collective-permute-done((f32[256,768]{1,0:T(8,128)S(1)}, f32[256,768]{1,0:T(8,128)S(1)}, u32[]{:S(2)}, u32[]{:S(2)}) %collective-permute-start.12) | collective-permute-done | bytes 786464 | tf_op jit(solution)/shard_map/ppermute | solution.py:17
  244.3 0.1 bitcast_dynamic-update-slice_fusion.3
  244.3 0.0 collective-permute-done.13
  244.3 0.1 bitcast_dynamic-update-slice_fusion.2
  244.4 0.0 collective-permute-done.14
  244.4 1.2 bitcast_dynamic-update-slice_fusion.1
  245.6 0.0 collective-permute-done.15
  245.6 1.2 bitcast_dynamic-update-slice_fusion
  246.8 9.6 %fusion = f32[16,256,768]{2,0,1:T(8,128)} fusion(f32[8,256,768]{2,1,0:T(8,128)S(1)} %bitcast_dynamic-update-slice_fusion, s32[8]{0:T(128)S(1)} %bitcast.66), kind=kOutput, calls=%fused_computation.5 | convolution fusion | flops 301990016 | bytes 18874400 | tf_op jit(solution)/shard_map/jb,jrd->brd/dot_general | solution.py:53
  256.5 16.8 %copy.9 = f32[16,256,768]{2,1,0:T(8,128)} copy(f32[16,256,768]{2,0,1:T(8,128)} %fusion) | data formatting | bytes 25165824 | tf_op jit(solution)/shard_map/jb,jrd->brd/dot_general | solution.py:53
  (23 shorter events, 0.3 us)
Async XLA Ops:
  0.6 68.7 %copy-start = (bf16[1024,768]{1,0:T(8,128)(2,1)S(1)}, bf16[1024,768]{1,0:T(8,128)(2,1)}, u32[]{:S(2)}) copy-start(bf16[1024,768]{1,0:T(8,128)(2,1)} %param.4) | copy-start | bytes 4718596
  7.3 13.0 %copy-start.6 = (s32[1024]{0:T(1024)S(1)}, s32[1024]{0:T(1024)}, u32[]{:S(2)}) copy-start(s32[1024]{0:T(1024)} %param.7) | copy-start | bytes 12292
  9.8 59.5 %collective-permute-start.7 = (bf16[256,768]{1,0:T(8,128)(2,1)S(1)}, bf16[256,768]{1,0:T(8,128)(2,1)S(1)}, u32[]{:S(2)}, u32[]{:S(2)}) collective-permute-start(bf16[256,768]{1,0:T(8,128)(2,1)S(1)} %get-tuple-element.13), channel_id=1, source_target_pairs={{0,113},{1,114},{2,115},{3,116},{4,117},{5,118},{6,119},{7,120},{8... | collective-permute-start | bytes 1179656 | tf_op jit(solution)/shard_map/ppermute | solution.py:17
  10.5 36.6 %collective-permute-start.3 = (bf16[256,768]{1,0:T(8,128)(2,1)S(1)}, bf16[256,768]{1,0:T(8,128)(2,1)S(1)}, u32[]{:S(2)}, u32[]{:S(2)}) collective-permute-start(bf16[256,768]{1,0:T(8,128)(2,1)S(1)} %get-tuple-element.17), channel_id=1, source_target_pairs={{0,49},{1,50},{2,51},{3,52},{4,53},{5,54},{6,55},{7,56},{8,57},{9,... | collective-permute-start | bytes 1179656 | tf_op jit(solution)/shard_map/ppermute | solution.py:17
  16.9 30.1 %collective-permute-start.2 = (bf16[256,768]{1,0:T(8,128)(2,1)S(1)}, bf16[256,768]{1,0:T(8,128)(2,1)S(1)}, u32[]{:S(2)}, u32[]{:S(2)}) collective-permute-start(bf16[256,768]{1,0:T(8,128)(2,1)S(1)} %get-tuple-element.18), channel_id=1, source_target_pairs={{0,33},{1,34},{2,35},{3,36},{4,37},{5,38},{6,39},{7,40},{8,41},{9,... | collective-permute-start | bytes 1179656 | tf_op jit(solution)/shard_map/ppermute | solution.py:17
  17.6 27.1 %collective-permute-start.1 = (bf16[256,768]{1,0:T(8,128)(2,1)S(1)}, bf16[256,768]{1,0:T(8,128)(2,1)S(1)}, u32[]{:S(2)}, u32[]{:S(2)}) collective-permute-start(bf16[256,768]{1,0:T(8,128)(2,1)S(1)} %get-tuple-element.19), channel_id=1, source_target_pairs={{0,17},{1,18},{2,19},{3,20},{4,21},{5,22},{6,23},{7,24},{8,25},{9,... | collective-permute-start | bytes 1179656 | tf_op jit(solution)/shard_map/ppermute | solution.py:17
  20.2 17.7 %collective-permute-start = (bf16[256,768]{1,0:T(8,128)(2,1)S(1)}, bf16[256,768]{1,0:T(8,128)(2,1)S(1)}, u32[]{:S(2)}, u32[]{:S(2)}) collective-permute-start(bf16[256,768]{1,0:T(8,128)(2,1)S(1)} %get-tuple-element.20), channel_id=1, source_target_pairs={{0,1},{1,2},{2,3},{3,4},{4,5},{5,6},{6,7},{7,8},{8,9},{9,10},{10,1... | collective-permute-start | bytes 1179656 | tf_op jit(solution)/shard_map/ppermute | solution.py:17
  37.9 11.8 %collective-permute-start.4 = (bf16[256,768]{1,0:T(8,128)(2,1)S(1)}, bf16[256,768]{1,0:T(8,128)(2,1)S(1)}, u32[]{:S(2)}, u32[]{:S(2)}) collective-permute-start(bf16[256,768]{1,0:T(8,128)(2,1)S(1)} %get-tuple-element.16), channel_id=1, source_target_pairs={{0,65},{1,66},{2,67},{3,68},{4,69},{5,70},{6,71},{7,72},{8,73},{9,... | collective-permute-start | bytes 1179656 | tf_op jit(solution)/shard_map/ppermute | solution.py:17
  44.7 18.7 %collective-permute-start.5 = (bf16[256,768]{1,0:T(8,128)(2,1)S(1)}, bf16[256,768]{1,0:T(8,128)(2,1)S(1)}, u32[]{:S(2)}, u32[]{:S(2)}) collective-permute-start(bf16[256,768]{1,0:T(8,128)(2,1)S(1)} %get-tuple-element.15), channel_id=1, source_target_pairs={{0,81},{1,82},{2,83},{3,84},{4,85},{5,86},{6,87},{7,88},{8,89},{9,... | collective-permute-start | bytes 1179656 | tf_op jit(solution)/shard_map/ppermute | solution.py:17
  47.0 22.3 %collective-permute-start.6 = (bf16[256,768]{1,0:T(8,128)(2,1)S(1)}, bf16[256,768]{1,0:T(8,128)(2,1)S(1)}, u32[]{:S(2)}, u32[]{:S(2)}) collective-permute-start(bf16[256,768]{1,0:T(8,128)(2,1)S(1)} %get-tuple-element.14), channel_id=1, source_target_pairs={{0,97},{1,98},{2,99},{3,100},{4,101},{5,102},{6,103},{7,104},{8,10... | collective-permute-start | bytes 1179656 | tf_op jit(solution)/shard_map/ppermute | solution.py:17
  69.3 3.6 %copy-start.4 = (bf16[2048,768]{1,0:T(8,128)(2,1)}, bf16[2048,768]{1,0:T(8,128)(2,1)S(1)}, u32[]{:S(2)}) copy-start(bf16[2048,768]{1,0:T(8,128)(2,1)S(1)} %constant_dynamic-update-slice_fusion) | copy-start | bytes 9437188
  73.0 3.4 %copy-start.2 = (f32[2048,1024]{1,0:T(8,128)}, f32[2048,1024]{1,0:T(8,128)S(1)}, u32[]{:S(2)}) copy-start(f32[2048,1024]{1,0:T(8,128)S(1)} %get-tuple-element.22) | copy-start | bytes 25165828
  127.9 5.7 %copy-start.3 = (f32[2048,1024]{1,0:T(8,128)S(1)}, f32[2048,1024]{1,0:T(8,128)}, u32[]{:S(2)}) copy-start(f32[2048,1024]{1,0:T(8,128)} %copy-done.2) | copy-start | bytes 25165828
  127.9 5.7 %copy-start.5 = (bf16[2048,768]{1,0:T(8,128)(2,1)S(1)}, bf16[2048,768]{1,0:T(8,128)(2,1)}, u32[]{:S(2)}) copy-start(bf16[2048,768]{1,0:T(8,128)(2,1)} %copy-done.4) | copy-start | bytes 9437188
  129.9 42.0 %collective-permute-start.10 = (f32[256,768]{1,0:T(8,128)}, f32[256,768]{1,0:T(8,128)}, u32[]{:S(2)}, u32[]{:S(2)}) collective-permute-start(f32[256,768]{1,0:T(8,128)} %get-tuple-element.10), channel_id=1, source_target_pairs={{0,95},{1,96},{2,97},{3,98},{4,99},{5,100},{6,101},{7,102},{8,103}... | collective-permute-start | bytes 2359304 | tf_op jit(solution)/shard_map/ppermute | solution.py:17
  129.9 40.7 %collective-permute-start.9 = (f32[256,768]{1,0:T(8,128)}, f32[256,768]{1,0:T(8,128)}, u32[]{:S(2)}, u32[]{:S(2)}) collective-permute-start(f32[256,768]{1,0:T(8,128)} %get-tuple-element.11), channel_id=1, source_target_pairs={{0,111},{1,112},{2,113},{3,114},{4,115},{5,116},{6,117},{7,118},{8... | collective-permute-start | bytes 2359304 | tf_op jit(solution)/shard_map/ppermute | solution.py:17
  133.6 30.7 %collective-permute-start.8 = (f32[256,768]{1,0:T(8,128)}, f32[256,768]{1,0:T(8,128)}, u32[]{:S(2)}, u32[]{:S(2)}) collective-permute-start(f32[256,768]{1,0:T(8,128)} %get-tuple-element.12), channel_id=1, source_target_pairs={{0,127},{1,0},{2,1},{3,2},{4,3},{5,4},{6,5},{7,6},{8,7},{9,8},{10,... | collective-permute-start | bytes 2359304 | tf_op jit(solution)/shard_map/ppermute | solution.py:17
  142.7 103.0 %collective-permute-start.15 = (f32[256,768]{1,0:T(8,128)S(1)}, f32[256,768]{1,0:T(8,128)}, u32[]{:S(2)}, u32[]{:S(2)}) collective-permute-start(f32[256,768]{1,0:T(8,128)S(1)} %get-tuple-element.5), channel_id=1, source_target_pairs={{0,15},{1,16},{2,17},{3,18},{4,19},{5,20},{6,21},{7,22},{8,23},{9,... | collective-permute-start | bytes 2359304 | tf_op jit(solution)/shard_map/ppermute | solution.py:17
  145.4 99.0 %collective-permute-start.14 = (f32[256,768]{1,0:T(8,128)S(1)}, f32[256,768]{1,0:T(8,128)}, u32[]{:S(2)}, u32[]{:S(2)}) collective-permute-start(f32[256,768]{1,0:T(8,128)S(1)} %get-tuple-element.6), channel_id=1, source_target_pairs={{0,31},{1,32},{2,33},{3,34},{4,35},{5,36},{6,37},{7,38},{8,39},{9,... | collective-permute-start | bytes 2359304 | tf_op jit(solution)/shard_map/ppermute | solution.py:17
  164.3 82.5 %copy-start.7 = (s32[1,8]{1,0:T(1,128)S(1)}, s32[1,8]{1,0:T(1,128)}, u32[]{:S(2)}) copy-start(s32[1,8]{1,0:T(1,128)} %param.6) | copy-start | bytes 100
  164.3 46.0 %collective-permute-start.11 = (f32[256,768]{1,0:T(8,128)}, f32[256,768]{1,0:T(8,128)S(1)}, u32[]{:S(2)}, u32[]{:S(2)}) collective-permute-start(f32[256,768]{1,0:T(8,128)} %get-tuple-element.9), channel_id=1, source_target_pairs={{0,79},{1,80},{2,81},{3,82},{4,83},{5,84},{6,85},{7,86},{8,87},{9,... | collective-permute-start | bytes 2359304 | tf_op jit(solution)/shard_map/ppermute | solution.py:17
  170.7 73.6 %collective-permute-start.12 = (f32[256,768]{1,0:T(8,128)S(1)}, f32[256,768]{1,0:T(8,128)S(1)}, u32[]{:S(2)}, u32[]{:S(2)}) collective-permute-start(f32[256,768]{1,0:T(8,128)S(1)} %get-tuple-element.8), channel_id=1, source_target_pairs={{0,63},{1,64},{2,65},{3,66},{4,67},{5,68},{6,69},{7,70},{8,71},{9,... | collective-permute-start | bytes 2359304 | tf_op jit(solution)/shard_map/ppermute | solution.py:17
  172.0 72.4 %collective-permute-start.13 = (f32[256,768]{1,0:T(8,128)S(1)}, f32[256,768]{1,0:T(8,128)S(1)}, u32[]{:S(2)}, u32[]{:S(2)}) collective-permute-start(f32[256,768]{1,0:T(8,128)S(1)} %get-tuple-element.7), channel_id=1, source_target_pairs={{0,47},{1,48},{2,49},{3,50},{4,51},{5,52},{6,53},{7,54},{8,55},{9,... | collective-permute-start | bytes 2359304 | tf_op jit(solution)/shard_map/ppermute | solution.py:17
  256.5 16.8 %copy-start.1 = (bf16[1024,768]{1,0:T(8,128)(2,1)S(1)}, bf16[1024,768]{1,0:T(8,128)(2,1)}, u32[]{:S(2)}) copy-start(bf16[1024,768]{1,0:T(8,128)(2,1)} %param.4) | copy-start | bytes 4718596
where the time goes:
time: 275 us; the launch traced here: 274 us
  waiting for transfers between devices  131 us (48%)
  local copies, waits for them, and re-layouts  47.5 us (17%)
  blocking collectives  32.6 us (12%)
  starting transfers between devices  28.8 us (10%)
  matrix products  25.8 us (9%)
  other arithmetic  5.53 us (2%)
    ppermute x16, waiting for transfers between devices, from_behind(): lax.ppermute(value, axis, [(i, (i + by) % length) for i in range(length)])  131 us
    psum x4, blocking collectives, over_axes(): return functools.reduce(lax.psum, axes, value)  32.6 us
    ppermute x16, starting transfers between devices, from_behind(): lax.ppermute(value, axis, [(i, (i + by) % length) for i in range(length)])  28.8 us
    dot_general x1, local copies, waits for them, and re-layouts, on_device(): jnp.einsum('jb,jrd->brd', selector, returned, precision=lax.Precision.HIG...  16.8 us
    gather x1, local copies, waits for them, and re-layouts, on_device(): target = jnp.take_along_axis(scores, gold[:, None], axis=1)[:, 0]  13.7 us
    dot_general x1, matrix products, on_device(): jnp.einsum('jb,jrd->brd', selector, returned, precision=lax.Precision.HIG...  9.64 us
    unnamed x31, local copies, waits for them, and re-layouts  8.52 us
    dot_general x1, matrix products, on_device(): lax.dot_general(dscore, mentions, (((0,), (0,)), ((), ())), preferred_ele...  6.72 us
  transfers between devices with their start and end apart: 16, of which 8 were waited for; matrix products, arithmetic and copies ran while one was open for 4% of the time, Pallas kernels for 0%

commit v1 on v0

v1 whole, which is shorter than its diff:
```python
import functools

import jax
import jax.numpy as jnp
from jax import lax
from jax.experimental import pallas as pl
from jax.experimental.pallas import tpu as pltpu
from jax.sharding import PartitionSpec as P

BLK = 256
ROUNDS = 8
MEN = 1024
D = 768
BPD = 16
N = 128
STRIDE = N // ROUNDS
STEPS = 8
ROWS = BLK // STEPS
AHEAD = 2
WIRE = jnp.bfloat16


def ring_peers(me):
    phases = []
    for weight, length in ((32, 4), (8, 4), (2, 4), (1, 2)):
        at = lax.rem(lax.div(me, weight), length)
        base = me - at * weight
        phases.append((at, [base + lax.rem(at + by, length) * weight for by in range(1, length)]))
    return phases


def exchange(
    picks, table, mentions, gold, ret, dm, loss,
    table_v, ment_v, send, cand, scores, dscore, gsend, dm_v, lsend, lbuf,
    local_sem, dm_sem, fsend, frecv, bsend, brecv, lsend_sem, lrecv_sem,
):
    me = lax.axis_index("ent")
    load_table = pltpu.make_async_copy(table, table_v, local_sem.at[0])
    load_table.start()
    load_mentions = pltpu.make_async_copy(mentions, ment_v, local_sem.at[1])
    load_mentions.start()

    ahead = [lax.rem(me + (j * STRIDE + 1), N) for j in range(ROUNDS)]
    behind = [lax.rem(me + (N - j * STRIDE - 1), N) for j in range(ROUNDS)]
    phases = ring_peers(me)
    peers = ahead + behind + [p for _, group in phases for p in group]
    barrier = pltpu.get_barrier_semaphore()
    for peer in peers:
        pl.semaphore_signal(barrier, inc=1, device_id=(peer,), device_id_type=pl.DeviceIdType.MESH)

    load_table.wait()
    for j in range(ROUNDS):
        send[j] = table_v[picks[0, j]]
    pl.semaphore_wait(barrier, len(peers))

    def forward(c, j):
        return pltpu.make_async_remote_copy(
            src_ref=send.at[j, pl.ds(pl.multiple_of(c * ROWS, ROWS), ROWS)],
            dst_ref=cand.at[c, pl.ds(j * ROWS, ROWS)],
            send_sem=fsend.at[c, j],
            recv_sem=frecv.at[c, j],
            device_id=(ahead[j],),
            device_id_type=pl.DeviceIdType.MESH,
        )

    def backward(c, j):
        return pltpu.make_async_remote_copy(
            src_ref=gsend.at[c, pl.ds(j * ROWS, ROWS)],
            dst_ref=ret.at[j, pl.ds(pl.multiple_of(c * ROWS, ROWS), ROWS)],
            send_sem=bsend.at[c, j],
            recv_sem=brecv.at[c, j],
            device_id=(behind[j],),
            device_id_type=pl.DeviceIdType.MESH,
        )

    for c in range(AHEAD):
        for j in range(ROUNDS):
            forward(c, j).start()

    load_mentions.wait()
    gold_row = jnp.concatenate([gold[r : r + 1, :] for r in range(MEN // 128)], axis=1)
    local = lax.broadcasted_iota(jnp.int32, (BLK, MEN), 0)
    spread = (local // ROWS) * BLK + local % ROWS

    def score_step(c, carry):
        top, total, target = carry
        for j in range(ROUNDS):
            forward(c, j).wait_recv()
        for j in range(ROUNDS):
            forward(c, j).wait_send()

        @pl.when(c + AHEAD < STEPS)
        def _():
            for j in range(ROUNDS):
                forward(c + AHEAD, j).start()

        scores[c] = lax.dot_general(
            cand[c], ment_v[...], (((1,), (1,)), ((), ())), preferred_element_type=jnp.float32
        )
        here = scores[c]
        newer = jnp.maximum(top, jnp.max(here, axis=0, keepdims=True))
        total = total * jnp.exp(top - newer) + jnp.sum(jnp.exp(here - newer), axis=0, keepdims=True)
        hit = spread == gold_row - c * ROWS
        target = target + jnp.sum(jnp.where(hit, here, 0.0), axis=0, keepdims=True)
        return newer, total, target

    row = (1, MEN)
    top, total, target = lax.fori_loop(
        0,
        STEPS,
        score_step,
        (
            jnp.full(row, -jnp.inf, jnp.float32),
            jnp.zeros(row, jnp.float32),
            jnp.zeros(row, jnp.float32),
        ),
    )
    lse = top + jnp.log(total)

    def start_phase(p, value):
        at, group = phases[p]
        lsend[p] = value
        lbuf[p, at] = value
        for d, peer in enumerate(group):
            loss_copy(p, d, at, peer).start()

    def loss_copy(p, d, at, peer):
        return pltpu.make_async_remote_copy(
            src_ref=lsend.at[p],
            dst_ref=lbuf.at[p, at],
            send_sem=lsend_sem.at[p, d],
            recv_sem=lrecv_sem.at[p, d],
            device_id=(peer,),
            device_id_type=pl.DeviceIdType.MESH,
        )

    def end_phase(p):
        at, group = phases[p]
        for d, peer in enumerate(group):
            loss_copy(p, d, at, peer).wait()
        value = lbuf[p, 0]
        for d in range(1, len(group) + 1):
            value = value + lbuf[p, d]
        return value

    start_phase(0, jnp.broadcast_to(jnp.sum(lse - target, axis=1, keepdims=True), (8, 128)))

    def gradient_step(c, _):
        hit = spread == gold_row - c * ROWS
        d = (jnp.exp(scores[c] - lse) - jnp.where(hit, 1.0, 0.0)).astype(jnp.bfloat16)
        dscore[c] = d
        gsend[c] = jnp.dot(d, ment_v[...], preferred_element_type=jnp.float32).astype(WIRE)

        @pl.when(c >= AHEAD)
        def _():
            for j in range(ROUNDS):
                backward(c - AHEAD, j).wait_send()

        for j in range(ROUNDS):
            backward(c, j).start()
        return 0

    lax.fori_loop(0, STEPS, gradient_step, 0)

    tiles = MEN // BLK
    for t in range(tiles):
        part = end_phase(t)
        if t + 1 < tiles:
            start_phase(t + 1, part)
        else:
            loss[...] = part
        columns = pl.ds(t * BLK, BLK)
        d = dscore[:, :, columns].reshape(STEPS * BLK, BLK)
        dm_v[columns, :] = lax.dot_general(
            d,
            cand[...].reshape(STEPS * BLK, D),
            (((0,), (0,)), ((), ())),
            preferred_element_type=jnp.float32,
        )
        pltpu.make_async_copy(dm_v.at[columns], dm.at[columns], dm_sem.at[t]).start()

    for t in range(tiles):
        columns = pl.ds(t * BLK, BLK)
        pltpu.make_async_copy(dm_v.at[columns], dm.at[columns], dm_sem.at[t]).wait()

    def finish(c, _):
        @pl.when(c >= STEPS - AHEAD)
        def _():
            for j in range(ROUNDS):
                backward(c, j).wait_send()

        for j in range(ROUNDS):
            backward(c, j).wait_recv()
        return 0

    lax.fori_loop(0, STEPS, finish, 0)


def collect(picks, ret, dm_in, loss_in, table_out, dm_out, loss_out, sem):
    b = pl.program_id(0)
    copy = pltpu.make_async_copy(dm_in, dm_out, sem)

    @pl.when(b == 0)
    def _():
        copy.start()
        loss_out[...] = loss_in[0:1, 0:1] * (1.0 / (N * MEN))

    table_out[...] = jnp.zeros_like(table_out)
    for j in range(ROUNDS):

        @pl.when(picks[0, j] == b)
        def _(j=j):
            table_out[...] += ret[j].astype(jnp.float32)

    @pl.when(b == BPD - 1)
    def _():
        copy.wait()


def on_device(mentions, table, picks, gold):
    vmem = pl.BlockSpec(memory_space=pltpu.VMEM)
    anywhere = pl.BlockSpec(memory_space=pl.ANY)
    ret, dm, loss = pl.pallas_call(
        exchange,
        out_shape=(
            jax.ShapeDtypeStruct((ROUNDS, BLK, D), WIRE),
            jax.ShapeDtypeStruct((MEN, D), jnp.float32),
            jax.ShapeDtypeStruct((8, 128), jnp.float32),
        ),
        in_specs=[pl.BlockSpec(memory_space=pltpu.SMEM), anywhere, anywhere, vmem],
        out_specs=(anywhere, anywhere, vmem),
        scratch_shapes=[
            pltpu.VMEM((BPD, BLK, D), jnp.bfloat16),
            pltpu.VMEM((MEN, D), jnp.bfloat16),
            pltpu.VMEM((ROUNDS, BLK, D), jnp.bfloat16),
            pltpu.VMEM((STEPS, BLK, D), jnp.bfloat16),
            pltpu.VMEM((STEPS, BLK, MEN), jnp.float32),
            pltpu.VMEM((STEPS, BLK, MEN), jnp.bfloat16),
            pltpu.VMEM((STEPS, BLK, D), WIRE),
            pltpu.VMEM((MEN, D), jnp.float32),
            pltpu.VMEM((4, 8, 128), jnp.float32),
            pltpu.VMEM((4, 4, 8, 128), jnp.float32),
            pltpu.SemaphoreType.DMA((2,)),
            pltpu.SemaphoreType.DMA((4,)),
            pltpu.SemaphoreType.DMA((STEPS, ROUNDS)),
            pltpu.SemaphoreType.DMA((STEPS, ROUNDS)),
            pltpu.SemaphoreType.DMA((STEPS, ROUNDS)),
            pltpu.SemaphoreType.DMA((STEPS, ROUNDS)),
            pltpu.SemaphoreType.DMA((4, 3)),
            pltpu.SemaphoreType.DMA((4, 3)),
        ],
        compiler_params=pltpu.CompilerParams(
            collective_id=0, has_side_effects=True, vmem_limit_bytes=56 * 2**20
        ),
        name="exchange",
    )(picks, table.reshape(BPD, BLK, D), mentions, gold.reshape(8, 128))
    d_table, d_mentions, total = pl.pallas_call(
        collect,
        grid=(BPD,),
        out_shape=(
            jax.ShapeDtypeStruct((BPD * BLK, D), jnp.float32),
            jax.ShapeDtypeStruct((MEN, D), jnp.float32),
            jax.ShapeDtypeStruct((1, 1), jnp.float32),
        ),
        in_specs=[
            pl.BlockSpec(memory_space=pltpu.SMEM),
            pl.BlockSpec((ROUNDS, BLK, D), lambda b: (0, 0, 0)),
            anywhere,
            pl.BlockSpec((8, 128), lambda b: (0, 0)),
        ],
        out_specs=(
            pl.BlockSpec((BLK, D), lambda b: (b, 0)),
            anywhere,
            pl.BlockSpec((1, 1), lambda b: (0, 0)),
        ),
        scratch_shapes=[pltpu.SemaphoreType.DMA],
        compiler_params=pltpu.CompilerParams(vmem_limit_bytes=32 * 2**20),
        name="collect",
    )(picks, ret, dm, loss)
    return total.reshape(()), d_mentions, d_table


def solution(mesh):
    return jax.shard_map(
        on_device,
        mesh=mesh,
        in_specs=(P("ent", None), P("ent", None), P("ent", None), P("ent")),
        out_specs=(P(), P("ent", None), P("ent", None)),
        check_vma=False,
    )
```

time: 275 us -> 110 us (0.40)
  the two profiles are of different devices: /device:TPU:24 before, /device:TPU:1 now
where the time goes in v1:
time: 110 us
  Pallas kernels  104 us (95%)
  local copies, waits for them, and re-layouts  4.46 us (4%)
    pallas_call x1, Pallas kernels, on_device(): pl.pallas_call(exchange, out_shape=(jax.ShapeDtypeStruct((ROUNDS, BLK, D)...  94.5 us
    pallas_call x1, Pallas kernels, on_device(): pl.pallas_call(collect, grid=(BPD,), out_shape=(jax.ShapeDtypeStruct((BPD...  9.88 us
    unnamed x8, local copies, waits for them, and re-layouts  4.46 us

profile of v1, /device:TPU:1, one launch (start us, length us, event | category | flops | bytes accessed | tf_op | source)
XLA Modules:
  0.0 109.5 jit_solution(16403638950512683794)
XLA Ops:
  0.6 0.0 copy-start.3
  0.6 94.5 %exchange.1 = (bf16[8,256,768]{2,1,0:T(8,128)(2,1)}, f32[1024,768]{1,0:T(8,128)}, f32[8,128]{1,0:T(8,128)}) custom-call(s32[1,8]{1,0:T(1,128)} %picks.3, bf16[16,256,768]{2,1,0:T(8,128)(2,1)} %bitcast.3, bf16[1024,768]{1,0:T(8,128)(2,1)} %mentions.1, s32[8,128]{1,0:T(8,128)} %bitcast.4), custom_call_target="tpu_custom_call" | custom-call | tf_op jit(solution)/shard_map/exchange/pallas_call | solution.py:223
  95.2 0.0 copy-done.3
  95.2 0.0 copy-start
  95.2 1.9 %copy-done = bf16[8,256,768]{2,1,0:T(8,128)(2,1)S(1)} copy-done((bf16[8,256,768]{2,1,0:T(8,128)(2,1)S(1)}, bf16[8,256,768]{2,1,0:T(8,128)(2,1)}, u32[]{:S(2)}) %copy-start) | copy-done | bytes 3145752
  97.1 0.0 copy-start.1
  97.1 1.9 %copy-done.1 = f32[1024,768]{1,0:T(8,128)S(1)} copy-done((f32[1024,768]{1,0:T(8,128)S(1)}, f32[1024,768]{1,0:T(8,128)}, u32[]{:S(2)}) %copy-start.1) | copy-done | bytes 3145752
  99.0 0.0 copy-start.2
  99.0 0.7 copy-done.2
  99.7 9.9 %collect.1 = (f32[4096,768]{1,0:T(8,128)}, f32[1024,768]{1,0:T(8,128)}, f32[1,1]{1,0:T(1,128)}) custom-call(s32[1,8]{1,0:T(1,128)S(1)} %copy-done.3, bf16[8,256,768]{2,1,0:T(8,128)(2,1)S(1)} %copy-done, f32[1024,768]{1,0:T(8,128)S(1)} %copy-done.1, f32[8,128]{1,0:T(8,128)S(1)} %copy-done.2), custom_call_target="tpu_custom_call" | custom-call | tf_op jit(solution)/shard_map/collect/pallas_call | solution.py:257
Async XLA Ops:
  0.6 94.6 %copy-start.3 = (s32[1,8]{1,0:T(1,128)S(1)}, s32[1,8]{1,0:T(1,128)}, u32[]{:S(2)}) copy-start(s32[1,8]{1,0:T(1,128)} %picks.3) | copy-start | bytes 100
  95.2 1.9 %copy-start = (bf16[8,256,768]{2,1,0:T(8,128)(2,1)S(1)}, bf16[8,256,768]{2,1,0:T(8,128)(2,1)}, u32[]{:S(2)}) copy-start(bf16[8,256,768]{2,1,0:T(8,128)(2,1)} %get-tuple-element.9.ret) | copy-start | bytes 9437188
  97.1 1.9 %copy-start.1 = (f32[1024,768]{1,0:T(8,128)S(1)}, f32[1024,768]{1,0:T(8,128)}, u32[]{:S(2)}) copy-start(f32[1024,768]{1,0:T(8,128)} %get-tuple-element.10.dm_in) | copy-start | bytes 9437188
  99.0 0.7 copy-start.2

commit v2 on v1

--- a/solution.py
+++ b/solution.py
@@ -16,7 +16,7 @@
 STRIDE = N // ROUNDS
 STEPS = 8
 ROWS = BLK // STEPS
-AHEAD = 2
+AHEAD = 4
 WIRE = jnp.bfloat16
 
 
@@ -31,8 +31,8 @@
 
 def exchange(
     picks, table, mentions, gold, ret, dm, loss,
-    table_v, ment_v, send, cand, scores, dscore, gsend, dm_v, lsend, lbuf,
-    local_sem, dm_sem, fsend, frecv, bsend, brecv, lsend_sem, lrecv_sem,
+    table_v, ment_v, send, cand, scores, dscore, gsend, lsend, lbuf,
+    local_sem, fsend, frecv, bsend, brecv, lsend_sem, lrecv_sem,
 ):
     me = lax.axis_index("ent")
     load_table = pltpu.make_async_copy(table, table_v, local_sem.at[0])
@@ -171,17 +171,12 @@
             loss[...] = part
         columns = pl.ds(t * BLK, BLK)
         d = dscore[:, :, columns].reshape(STEPS * BLK, BLK)
-        dm_v[columns, :] = lax.dot_general(
+        dm[columns, :] = lax.dot_general(
             d,
             cand[...].reshape(STEPS * BLK, D),
             (((0,), (0,)), ((), ())),
             preferred_element_type=jnp.float32,
         )
-        pltpu.make_async_copy(dm_v.at[columns], dm.at[columns], dm_sem.at[t]).start()
-
-    for t in range(tiles):
-        columns = pl.ds(t * BLK, BLK)
-        pltpu.make_async_copy(dm_v.at[columns], dm.at[columns], dm_sem.at[t]).wait()
 
     def finish(c, _):
         @pl.when(c >= STEPS - AHEAD)
@@ -196,25 +191,57 @@
     lax.fori_loop(0, STEPS, finish, 0)
 
 
-def collect(picks, ret, dm_in, loss_in, table_out, dm_out, loss_out, sem):
-    b = pl.program_id(0)
-    copy = pltpu.make_async_copy(dm_in, dm_out, sem)
-
-    @pl.when(b == 0)
-    def _():
-        copy.start()
-        loss_out[...] = loss_in[0:1, 0:1] * (1.0 / (N * MEN))
-
-    table_out[...] = jnp.zeros_like(table_out)
+def collect(picks, ret, dm_in, loss_in, table_out, dm_out, loss_out, zero, acc, dm_sem, zero_sem, acc_sem):
+    dm_copy = pltpu.make_async_copy(dm_in, dm_out, dm_sem)
+    dm_copy.start()
+    zero[...] = jnp.zeros_like(zero)
+    picked = [picks[0, j] for j in range(ROUNDS)]
+
+    def clear(b):
+        return pltpu.make_async_copy(zero, table_out.at[b], zero_sem.at[b])
+
+    def store(j):
+        return pltpu.make_async_copy(acc.at[j], table_out.at[picked[j]], acc_sem.at[j])
+
+    def unused(b):
+        return functools.reduce(jnp.logical_and, [p != b for p in picked])
+
+    def first(j):
+        return functools.reduce(jnp.logical_and, [picked[i] != picked[j] for i in range(j)], True)
+
+    for b in range(BPD):
+
+        @pl.when(unused(b))
+        def _(b=b):
+            clear(b).start()
+
     for j in range(ROUNDS):
 
-        @pl.when(picks[0, j] == b)
+        @pl.when(first(j))
         def _(j=j):
-            table_out[...] += ret[j].astype(jnp.float32)
-
-    @pl.when(b == BPD - 1)
-    def _():
-        copy.wait()
+            acc[j] = ret[j].astype(jnp.float32)
+            for i in range(j + 1, ROUNDS):
+
+                @pl.when(picked[i] == picked[j])
+                def _(i=i):
+                    acc[j] += ret[i].astype(jnp.float32)
+
+            store(j).start()
+
+    loss_out[...] = loss_in[0:1, 0:1] * (1.0 / (N * MEN))
+    for b in range(BPD):
+
+        @pl.when(unused(b))
+        def _(b=b):
+            clear(b).wait()
+
+    for j in range(ROUNDS):
+
+        @pl.when(first(j))
+        def _(j=j):
+            store(j).wait()
+
+    dm_copy.wait()
 
 
 def on_device(mentions, table, picks, gold):
@@ -223,12 +250,12 @@
     ret, dm, loss = pl.pallas_call(
         exchange,
         out_shape=(
-            jax.ShapeDtypeStruct((ROUNDS, BLK, D), WIRE),
-            jax.ShapeDtypeStruct((MEN, D), jnp.float32),
-            jax.ShapeDtypeStruct((8, 128), jnp.float32),
+            pltpu.VMEM((ROUNDS, BLK, D), WIRE),
+            pltpu.VMEM((MEN, D), jnp.float32),
+            pltpu.VMEM((8, 128), jnp.float32),
         ),
         in_specs=[pl.BlockSpec(memory_space=pltpu.SMEM), anywhere, anywhere, vmem],
-        out_specs=(anywhere, anywhere, vmem),
+        out_specs=(vmem, vmem, vmem),
         scratch_shapes=[
             pltpu.VMEM((BPD, BLK, D), jnp.bfloat16),
             pltpu.VMEM((MEN, D), jnp.bfloat16),
@@ -237,11 +264,9 @@
             pltpu.VMEM((STEPS, BLK, MEN), jnp.float32),
             pltpu.VMEM((STEPS, BLK, MEN), jnp.bfloat16),
             pltpu.VMEM((STEPS, BLK, D), WIRE),
-            pltpu.VMEM((MEN, D), jnp.float32),
             pltpu.VMEM((4, 8, 128), jnp.float32),
             pltpu.VMEM((4, 4, 8, 128), jnp.float32),
             pltpu.SemaphoreType.DMA((2,)),
-            pltpu.SemaphoreType.DMA((4,)),
             pltpu.SemaphoreType.DMA((STEPS, ROUNDS)),
             pltpu.SemaphoreType.DMA((STEPS, ROUNDS)),
             pltpu.SemaphoreType.DMA((STEPS, ROUNDS)),
@@ -256,28 +281,24 @@
     )(picks, table.reshape(BPD, BLK, D), mentions, gold.reshape(8, 128))
     d_table, d_mentions, total = pl.pallas_call(
         collect,
-        grid=(BPD,),
         out_shape=(
-            jax.ShapeDtypeStruct((BPD * BLK, D), jnp.float32),
+            jax.ShapeDtypeStruct((BPD, BLK, D), jnp.float32),
             jax.ShapeDtypeStruct((MEN, D), jnp.float32),
             jax.ShapeDtypeStruct((1, 1), jnp.float32),
         ),
-        in_specs=[
-            pl.BlockSpec(memory_space=pltpu.SMEM),
-            pl.BlockSpec((ROUNDS, BLK, D), lambda b: (0, 0, 0)),
-            anywhere,
-            pl.BlockSpec((8, 128), lambda b: (0, 0)),
+        in_specs=[pl.BlockSpec(memory_space=pltpu.SMEM), vmem, vmem, vmem],
+        out_specs=(anywhere, anywhere, vmem),
+        scratch_shapes=[
+            pltpu.VMEM((BLK, D), jnp.float32),
+            pltpu.VMEM((ROUNDS, BLK, D), jnp.float32),
+            pltpu.SemaphoreType.DMA,
+            pltpu.SemaphoreType.DMA((BPD,)),
+            pltpu.SemaphoreType.DMA((ROUNDS,)),
         ],
-        out_specs=(
-            pl.BlockSpec((BLK, D), lambda b: (b, 0)),
-            anywhere,
-            pl.BlockSpec((1, 1), lambda b: (0, 0)),
-        ),
-        scratch_shapes=[pltpu.SemaphoreType.DMA],
-        compiler_params=pltpu.CompilerParams(vmem_limit_bytes=32 * 2**20),
+        compiler_params=pltpu.CompilerParams(vmem_limit_bytes=24 * 2**20),
         name="collect",
     )(picks, ret, dm, loss)
-    return total.reshape(()), d_mentions, d_table
+    return total.reshape(()), d_mentions, d_table.reshape(BPD * BLK, D)
 
 
 def solution(mesh):

time: 110 us -> 99.5 us (0.905)
  Pallas kernels: 104 us -> 98.7 us
  local copies, waits for them, and re-layouts: 4.46 us -> 0.01 us
    pallas_call x2, Pallas kernels: 104 us -> 98.7 us  [the longest x1 91.9 us: on_device(): pl.pallas_call(exchange, out_shape=(pltpu.VMEM((ROUNDS, BLK, D), WIRE), p...]
    unnamed x8 -> x2, local copies, waits for them, and re-layouts: 4.46 us -> 0.01 us
where the time goes in v2:
time: 99.5 us; the launch traced here: 99.4 us
  Pallas kernels  98.7 us (99%)
    pallas_call x1, Pallas kernels, on_device(): pl.pallas_call(exchange, out_shape=(pltpu.VMEM((ROUNDS, BLK, D), WIRE), p...  91.9 us
    pallas_call x1, Pallas kernels, on_device(): pl.pallas_call(collect, out_shape=(jax.ShapeDtypeStruct((BPD, BLK, D), jn...  6.83 us

profile of v2, /device:TPU:1, one launch (start us, length us, event | category | flops | bytes accessed | tf_op | source)
XLA Modules:
  0.0 99.4 jit_solution(4231456703246886230)
XLA Ops:
  0.6 0.0 copy-start
  0.6 91.9 %exchange.1 = (bf16[8,256,768]{2,1,0:T(8,128)(2,1)S(1)}, f32[1024,768]{1,0:T(8,128)S(1)}, f32[8,128]{1,0:T(8,128)S(1)}) custom-call(s32[1,8]{1,0:T(1,128)} %picks.3, bf16[16,256,768]{2,1,0:T(8,128)(2,1)} %bitcast.4, bf16[1024,768]{1,0:T(8,128)(2,1)} %mentions.1, s32[8,128]{1,0:T(8,128)} %bitcast.5), custom_call_target="tpu_custom_call" | custom-call | tf_op jit(solution)/shard_map/exchange/pallas_call | solution.py:250
  92.6 0.0 copy-done
  92.6 6.8 %collect.1 = (f32[16,256,768]{2,1,0:T(8,128)}, f32[1024,768]{1,0:T(8,128)}, f32[1,1]{1,0:T(1,128)}) custom-call(s32[1,8]{1,0:T(1,128)S(1)} %copy-done, bf16[8,256,768]{2,1,0:T(8,128)(2,1)S(1)} %get-tuple-element.9.ret, f32[1024,768]{1,0:T(8,128)S(1)} %get-tuple-element.10.dm_in, f32[8,128]{1,0:T(8,128)S(1)} %get-tuple-element.11.loss_in), custom_call_target="tpu_custom_call" | custom-call | tf_op jit(solution)/shard_map/collect/pallas_call | solution.py:282
Async XLA Ops:
  0.6 91.9 %copy-start = (s32[1,8]{1,0:T(1,128)S(1)}, s32[1,8]{1,0:T(1,128)}, u32[]{:S(2)}) copy-start(s32[1,8]{1,0:T(1,128)} %picks.3) | copy-start | bytes 100

commit v3 on v2

--- a/solution.py
+++ b/solution.py
@@ -17,6 +17,7 @@
 STEPS = 8
 ROWS = BLK // STEPS
 AHEAD = 4
+WINDOW = 8
 WIRE = jnp.bfloat16
 
 
@@ -31,14 +32,20 @@
 
 def exchange(
     picks, table, mentions, gold, ret, dm, loss,
-    table_v, ment_v, send, cand, scores, dscore, gsend, lsend, lbuf,
+    part_a, part_b, part_c, part_d, ment_v, gold_v, send, cand, scores, dscore, gsend, lsend, lbuf,
     local_sem, fsend, frecv, bsend, brecv, lsend_sem, lrecv_sem,
 ):
     me = lax.axis_index("ent")
-    load_table = pltpu.make_async_copy(table, table_v, local_sem.at[0])
-    load_table.start()
-    load_mentions = pltpu.make_async_copy(mentions, ment_v, local_sem.at[1])
-    load_mentions.start()
+    parts = (part_a, part_b, part_c, part_d)
+    depth = BLK // len(parts)
+    loads = [
+        pltpu.make_async_copy(table.at[:, pl.ds(q * depth, depth)], part, local_sem.at[q])
+        for q, part in enumerate(parts)
+    ]
+    load_mentions = pltpu.make_async_copy(mentions, ment_v, local_sem.at[len(parts)])
+    load_gold = pltpu.make_async_copy(gold, gold_v, local_sem.at[len(parts) + 1])
+    for load in loads:
+        load.start()
 
     ahead = [lax.rem(me + (j * STRIDE + 1), N) for j in range(ROUNDS)]
     behind = [lax.rem(me + (N - j * STRIDE - 1), N) for j in range(ROUNDS)]
@@ -47,52 +54,68 @@
     barrier = pltpu.get_barrier_semaphore()
     for peer in peers:
         pl.semaphore_signal(barrier, inc=1, device_id=(peer,), device_id_type=pl.DeviceIdType.MESH)
-
-    load_table.wait()
-    for j in range(ROUNDS):
-        send[j] = table_v[picks[0, j]]
-    pl.semaphore_wait(barrier, len(peers))
-
-    def forward(c, j):
+    load_mentions.start()
+    load_gold.start()
+
+    def remote(src, dst, send_sem, recv_sem, device):
         return pltpu.make_async_remote_copy(
-            src_ref=send.at[j, pl.ds(pl.multiple_of(c * ROWS, ROWS), ROWS)],
-            dst_ref=cand.at[c, pl.ds(j * ROWS, ROWS)],
-            send_sem=fsend.at[c, j],
-            recv_sem=frecv.at[c, j],
-            device_id=(ahead[j],),
+            src_ref=src,
+            dst_ref=dst,
+            send_sem=send_sem,
+            recv_sem=recv_sem,
+            device_id=(device,),
             device_id_type=pl.DeviceIdType.MESH,
         )
 
-    def backward(c, j):
-        return pltpu.make_async_remote_copy(
-            src_ref=gsend.at[c, pl.ds(j * ROWS, ROWS)],
-            dst_ref=ret.at[j, pl.ds(pl.multiple_of(c * ROWS, ROWS), ROWS)],
-            send_sem=bsend.at[c, j],
-            recv_sem=brecv.at[c, j],
-            device_id=(behind[j],),
-            device_id_type=pl.DeviceIdType.MESH,
-        )
-
-    for c in range(AHEAD):
+    def wait_for(ref, sem):
+        pltpu.make_async_copy(ref, ref, sem).wait()
+
+    def start_forward(c):
         for j in range(ROUNDS):
-            forward(c, j).start()
+            remote(
+                send.at[c, pl.ds(j * ROWS, ROWS)],
+                cand.at[c, pl.ds(j * ROWS, ROWS)],
+                fsend.at[c],
+                frecv.at[c],
+                ahead[j],
+            ).start()
+
+    def start_backward(c):
+        for j in range(ROUNDS):
+            remote(
+                gsend.at[c, pl.ds(j * ROWS, ROWS)],
+                ret.at[j, pl.ds(pl.multiple_of(c * ROWS, ROWS), ROWS)],
+                bsend.at[c],
+                brecv.at[0],
+                behind[j],
+            ).start()
+
+    for q, part in enumerate(parts):
+        loads[q].wait()
+        for j in range(ROUNDS):
+            block = part[picks[0, j]]
+            for h in range(depth // ROWS):
+                send[q * (depth // ROWS) + h, j * ROWS : (j + 1) * ROWS] = block[h * ROWS : (h + 1) * ROWS]
+        if q == 0:
+            pl.semaphore_wait(barrier, len(peers))
+        for c in range(q * (depth // ROWS), (q + 1) * (depth // ROWS)):
+            if c < AHEAD:
+                start_forward(c)
 
     load_mentions.wait()
-    gold_row = jnp.concatenate([gold[r : r + 1, :] for r in range(MEN // 128)], axis=1)
+    load_gold.wait()
+    gold_row = jnp.concatenate([gold_v[r : r + 1, :] for r in range(MEN // 128)], axis=1)
     local = lax.broadcasted_iota(jnp.int32, (BLK, MEN), 0)
     spread = (local // ROWS) * BLK + local % ROWS
 
     def score_step(c, carry):
         top, total, target = carry
-        for j in range(ROUNDS):
-            forward(c, j).wait_recv()
-        for j in range(ROUNDS):
-            forward(c, j).wait_send()
+        wait_for(cand.at[c], frecv.at[c])
+        wait_for(send.at[c], fsend.at[c])
 
         @pl.when(c + AHEAD < STEPS)
         def _():
-            for j in range(ROUNDS):
-                forward(c + AHEAD, j).start()
+            start_forward(c + AHEAD)
 
         scores[c] = lax.dot_general(
             cand[c], ment_v[...], (((1,), (1,)), ((), ())), preferred_element_type=jnp.float32
@@ -117,78 +140,56 @@
     )
     lse = top + jnp.log(total)
 
-    def start_phase(p, value):
-        at, group = phases[p]
-        lsend[p] = value
-        lbuf[p, at] = value
-        for d, peer in enumerate(group):
-            loss_copy(p, d, at, peer).start()
-
-    def loss_copy(p, d, at, peer):
-        return pltpu.make_async_remote_copy(
-            src_ref=lsend.at[p],
-            dst_ref=lbuf.at[p, at],
-            send_sem=lsend_sem.at[p, d],
-            recv_sem=lrecv_sem.at[p, d],
-            device_id=(peer,),
-            device_id_type=pl.DeviceIdType.MESH,
-        )
-
-    def end_phase(p):
-        at, group = phases[p]
-        for d, peer in enumerate(group):
-            loss_copy(p, d, at, peer).wait()
-        value = lbuf[p, 0]
-        for d in range(1, len(group) + 1):
-            value = value + lbuf[p, d]
-        return value
-
-    start_phase(0, jnp.broadcast_to(jnp.sum(lse - target, axis=1, keepdims=True), (8, 128)))
-
     def gradient_step(c, _):
         hit = spread == gold_row - c * ROWS
         d = (jnp.exp(scores[c] - lse) - jnp.where(hit, 1.0, 0.0)).astype(jnp.bfloat16)
         dscore[c] = d
         gsend[c] = jnp.dot(d, ment_v[...], preferred_element_type=jnp.float32).astype(WIRE)
 
-        @pl.when(c >= AHEAD)
+        @pl.when(c >= WINDOW)
         def _():
-            for j in range(ROUNDS):
-                backward(c - AHEAD, j).wait_send()
-
-        for j in range(ROUNDS):
-            backward(c, j).start()
+            wait_for(gsend.at[c - WINDOW], bsend.at[c - WINDOW])
+
+        start_backward(c)
         return 0
 
     lax.fori_loop(0, STEPS, gradient_step, 0)
 
+    def start_phase(p, value):
+        at, group = phases[p]
+        lsend[p] = value
+        lbuf[p, at] = value
+        for peer in group:
+            remote(lsend.at[p], lbuf.at[p, at], lsend_sem.at[p], lrecv_sem.at[p], peer).start()
+
+    def end_phase(p):
+        count = len(phases[p][1])
+        wait_for(lbuf.at[p, pl.ds(0, count)], lsend_sem.at[p])
+        wait_for(lbuf.at[p, pl.ds(0, count)], lrecv_sem.at[p])
+        value = lbuf[p, 0]
+        for d in range(1, count + 1):
+            value = value + lbuf[p, d]
+        return value
+
+    start_phase(0, jnp.broadcast_to(jnp.sum(lse - target, axis=1, keepdims=True), (8, 128)))
     tiles = MEN // BLK
     for t in range(tiles):
+        columns = pl.ds(t * BLK, BLK)
+        dm[columns, :] = lax.dot_general(
+            dscore[:, :, columns].reshape(STEPS * BLK, BLK),
+            cand[...].reshape(STEPS * BLK, D),
+            (((0,), (0,)), ((), ())),
+            preferred_element_type=jnp.float32,
+        )
         part = end_phase(t)
         if t + 1 < tiles:
             start_phase(t + 1, part)
         else:
             loss[...] = part
-        columns = pl.ds(t * BLK, BLK)
-        d = dscore[:, :, columns].reshape(STEPS * BLK, BLK)
-        dm[columns, :] = lax.dot_general(
-            d,
-            cand[...].reshape(STEPS * BLK, D),
-            (((0,), (0,)), ((), ())),
-            preferred_element_type=jnp.float32,
-        )
-
-    def finish(c, _):
-        @pl.when(c >= STEPS - AHEAD)
-        def _():
-            for j in range(ROUNDS):
-                backward(c, j).wait_send()
-
-        for j in range(ROUNDS):
-            backward(c, j).wait_recv()
-        return 0
-
-    lax.fori_loop(0, STEPS, finish, 0)
+
+    for c in range(STEPS - WINDOW, STEPS):
+        wait_for(gsend.at[c], bsend.at[c])
+    wait_for(ret, brecv.at[0])
 
 
 def collect(picks, ret, dm_in, loss_in, table_out, dm_out, loss_out, zero, acc, dm_sem, zero_sem, acc_sem):
@@ -254,25 +255,26 @@
             pltpu.VMEM((MEN, D), jnp.float32),
             pltpu.VMEM((8, 128), jnp.float32),
         ),
-        in_specs=[pl.BlockSpec(memory_space=pltpu.SMEM), anywhere, anywhere, vmem],
+        in_specs=[pl.BlockSpec(memory_space=pltpu.SMEM), anywhere, anywhere, anywhere],
         out_specs=(vmem, vmem, vmem),
         scratch_shapes=[
-            pltpu.VMEM((BPD, BLK, D), jnp.bfloat16),
+            *(pltpu.VMEM((BPD, BLK // 4, D), jnp.bfloat16) for _ in range(4)),
             pltpu.VMEM((MEN, D), jnp.bfloat16),
-            pltpu.VMEM((ROUNDS, BLK, D), jnp.bfloat16),
+            pltpu.VMEM((8, 128), jnp.int32),
+            pltpu.VMEM((STEPS, BLK, D), jnp.bfloat16),
             pltpu.VMEM((STEPS, BLK, D), jnp.bfloat16),
             pltpu.VMEM((STEPS, BLK, MEN), jnp.float32),
             pltpu.VMEM((STEPS, BLK, MEN), jnp.bfloat16),
             pltpu.VMEM((STEPS, BLK, D), WIRE),
             pltpu.VMEM((4, 8, 128), jnp.float32),
             pltpu.VMEM((4, 4, 8, 128), jnp.float32),
-            pltpu.SemaphoreType.DMA((2,)),
-            pltpu.SemaphoreType.DMA((STEPS, ROUNDS)),
-            pltpu.SemaphoreType.DMA((STEPS, ROUNDS)),
-            pltpu.SemaphoreType.DMA((STEPS, ROUNDS)),
-            pltpu.SemaphoreType.DMA((STEPS, ROUNDS)),
-            pltpu.SemaphoreType.DMA((4, 3)),
-            pltpu.SemaphoreType.DMA((4, 3)),
+            pltpu.SemaphoreType.DMA((6,)),
+            pltpu.SemaphoreType.DMA((STEPS,)),
+            pltpu.SemaphoreType.DMA((STEPS,)),
+            pltpu.SemaphoreType.DMA((STEPS,)),
+            pltpu.SemaphoreType.DMA((1,)),
+            pltpu.SemaphoreType.DMA((4,)),
+            pltpu.SemaphoreType.DMA((4,)),
         ],
         compiler_params=pltpu.CompilerParams(
             collective_id=0, has_side_effects=True, vmem_limit_bytes=56 * 2**20

time: 99.5 us -> 97.5 us (0.980)
  Pallas kernels: 98.7 us -> 96.8 us
    pallas_call x1, Pallas kernels: 91.9 us -> 89.9 us  [on_device(): pl.pallas_call(exchange, out_shape=(pltpu.VMEM((ROUNDS, BLK, D), WIRE), p...]
where the time goes in v3:
time: 97.5 us; the launch traced here: 97.4 us
  Pallas kernels  96.8 us (99%)
    pallas_call x1, Pallas kernels, on_device(): pl.pallas_call(exchange, out_shape=(pltpu.VMEM((ROUNDS, BLK, D), WIRE), p...  89.9 us
    pallas_call x1, Pallas kernels, on_device(): pl.pallas_call(collect, out_shape=(jax.ShapeDtypeStruct((BPD, BLK, D), jn...  6.83 us

profile of v3, /device:TPU:1, one launch (start us, length us, event | category | flops | bytes accessed | tf_op | source)
XLA Modules:
  0.0 97.4 jit_solution(16085728040771216973)
XLA Ops:
  0.6 0.0 copy-start
  0.6 89.9 %exchange.1 = (bf16[8,256,768]{2,1,0:T(8,128)(2,1)S(1)}, f32[1024,768]{1,0:T(8,128)S(1)}, f32[8,128]{1,0:T(8,128)S(1)}) custom-call(s32[1,8]{1,0:T(1,128)} %picks.3, bf16[16,256,768]{2,1,0:T(8,128)(2,1)} %bitcast.4, bf16[1024,768]{1,0:T(8,128)(2,1)} %mentions.1, s32[8,128]{1,0:T(8,128)} %bitcast.5), custom_call_target="tpu_custom_call" | custom-call | tf_op jit(solution)/shard_map/exchange/pallas_call | solution.py:251
  90.6 0.0 copy-done
  90.6 6.8 %collect.1 = (f32[16,256,768]{2,1,0:T(8,128)}, f32[1024,768]{1,0:T(8,128)}, f32[1,1]{1,0:T(1,128)}) custom-call(s32[1,8]{1,0:T(1,128)S(1)} %copy-done, bf16[8,256,768]{2,1,0:T(8,128)(2,1)S(1)} %get-tuple-element.9.ret, f32[1024,768]{1,0:T(8,128)S(1)} %get-tuple-element.10.dm_in, f32[8,128]{1,0:T(8,128)S(1)} %get-tuple-element.11.loss_in), custom_call_target="tpu_custom_call" | custom-call | tf_op jit(solution)/shard_map/collect/pallas_call | solution.py:284
Async XLA Ops:
  0.6 89.9 %copy-start = (s32[1,8]{1,0:T(1,128)S(1)}, s32[1,8]{1,0:T(1,128)}, u32[]{:S(2)}) copy-start(s32[1,8]{1,0:T(1,128)} %picks.3) | copy-start | bytes 100

commit v4 on v3

--- a/solution.py
+++ b/solution.py
@@ -17,7 +17,6 @@
 STEPS = 8
 ROWS = BLK // STEPS
 AHEAD = 4
-WINDOW = 8
 WIRE = jnp.bfloat16
 
 
@@ -80,12 +79,12 @@
                 ahead[j],
             ).start()
 
-    def start_backward(c):
-        for j in range(ROUNDS):
+    def start_backward(c, which):
+        for j in which:
             remote(
                 gsend.at[c, pl.ds(j * ROWS, ROWS)],
                 ret.at[j, pl.ds(pl.multiple_of(c * ROWS, ROWS), ROWS)],
-                bsend.at[c],
+                bsend.at[0],
                 brecv.at[0],
                 behind[j],
             ).start()
@@ -109,12 +108,12 @@
     spread = (local // ROWS) * BLK + local % ROWS
 
     def score_step(c, carry):
-        top, total, target = carry
+        top, total = carry
         wait_for(cand.at[c], frecv.at[c])
-        wait_for(send.at[c], fsend.at[c])
 
         @pl.when(c + AHEAD < STEPS)
         def _():
+            wait_for(send.at[c], fsend.at[c])
             start_forward(c + AHEAD)
 
         scores[c] = lax.dot_general(
@@ -123,37 +122,32 @@
         here = scores[c]
         newer = jnp.maximum(top, jnp.max(here, axis=0, keepdims=True))
         total = total * jnp.exp(top - newer) + jnp.sum(jnp.exp(here - newer), axis=0, keepdims=True)
-        hit = spread == gold_row - c * ROWS
-        target = target + jnp.sum(jnp.where(hit, here, 0.0), axis=0, keepdims=True)
-        return newer, total, target
+        return newer, total
 
     row = (1, MEN)
-    top, total, target = lax.fori_loop(
+    top, total = lax.fori_loop(
         0,
         STEPS,
         score_step,
         (
             jnp.full(row, -jnp.inf, jnp.float32),
             jnp.zeros(row, jnp.float32),
-            jnp.zeros(row, jnp.float32),
         ),
     )
     lse = top + jnp.log(total)
 
-    def gradient_step(c, _):
+    def gradient_step(c, target):
+        half = BLK // 2
         hit = spread == gold_row - c * ROWS
-        d = (jnp.exp(scores[c] - lse) - jnp.where(hit, 1.0, 0.0)).astype(jnp.bfloat16)
-        dscore[c] = d
-        gsend[c] = jnp.dot(d, ment_v[...], preferred_element_type=jnp.float32).astype(WIRE)
-
-        @pl.when(c >= WINDOW)
-        def _():
-            wait_for(gsend.at[c - WINDOW], bsend.at[c - WINDOW])
-
-        start_backward(c)
-        return 0
-
-    lax.fori_loop(0, STEPS, gradient_step, 0)
+        for h in range(2):
+            rows = slice(h * half, (h + 1) * half)
+            d = (jnp.exp(scores[c, rows] - lse) - jnp.where(hit[rows], 1.0, 0.0)).astype(jnp.bfloat16)
+            dscore[c, rows] = d
+            gsend[c, rows] = jnp.dot(d, ment_v[...], preferred_element_type=jnp.float32).astype(WIRE)
+            start_backward(c, range(h * ROUNDS // 2, (h + 1) * ROUNDS // 2))
+        return target + jnp.sum(jnp.where(hit, scores[c], 0.0), axis=0, keepdims=True)
+
+    target = lax.fori_loop(0, STEPS, gradient_step, jnp.zeros(row, jnp.float32))
 
     def start_phase(p, value):
         at, group = phases[p]
@@ -187,8 +181,9 @@
         else:
             loss[...] = part
 
-    for c in range(STEPS - WINDOW, STEPS):
-        wait_for(gsend.at[c], bsend.at[c])
+    for c in range(STEPS - AHEAD, STEPS):
+        wait_for(send.at[c], fsend.at[c])
+    wait_for(gsend, bsend.at[0])
     wait_for(ret, brecv.at[0])
 
 
@@ -271,7 +266,7 @@
             pltpu.SemaphoreType.DMA((6,)),
             pltpu.SemaphoreType.DMA((STEPS,)),
             pltpu.SemaphoreType.DMA((STEPS,)),
-            pltpu.SemaphoreType.DMA((STEPS,)),
+            pltpu.SemaphoreType.DMA((1,)),
             pltpu.SemaphoreType.DMA((1,)),
             pltpu.SemaphoreType.DMA((4,)),
             pltpu.SemaphoreType.DMA((4,)),

time: 97.5 us -> 97.3 us (level)
  no operation moved by 1% of the time
where the time goes in v4:
time: 97.3 us; the launch traced here: 97.2 us
  Pallas kernels  96.6 us (99%)
    pallas_call x1, Pallas kernels, on_device(): pl.pallas_call(exchange, out_shape=(pltpu.VMEM((ROUNDS, BLK, D), WIRE), p...  89.7 us
    pallas_call x1, Pallas kernels, on_device(): pl.pallas_call(collect, out_shape=(jax.ShapeDtypeStruct((BPD, BLK, D), jn...  6.83 us

profile of v4, /device:TPU:1, one launch (start us, length us, event | category | flops | bytes accessed | tf_op | source)
XLA Modules:
  0.0 97.2 jit_solution(2893700253179339429)
XLA Ops:
  0.6 0.0 copy-start
  0.6 89.7 %exchange.1 = (bf16[8,256,768]{2,1,0:T(8,128)(2,1)S(1)}, f32[1024,768]{1,0:T(8,128)S(1)}, f32[8,128]{1,0:T(8,128)S(1)}) custom-call(s32[1,8]{1,0:T(1,128)} %picks.3, bf16[16,256,768]{2,1,0:T(8,128)(2,1)} %bitcast.4, bf16[1024,768]{1,0:T(8,128)(2,1)} %mentions.1, s32[8,128]{1,0:T(8,128)} %bitcast.5), custom_call_target="tpu_custom_call" | custom-call | tf_op jit(solution)/shard_map/exchange/pallas_call | solution.py:246
  90.4 0.0 copy-done
  90.4 6.8 %collect.1 = (f32[16,256,768]{2,1,0:T(8,128)}, f32[1024,768]{1,0:T(8,128)}, f32[1,1]{1,0:T(1,128)}) custom-call(s32[1,8]{1,0:T(1,128)S(1)} %copy-done, bf16[8,256,768]{2,1,0:T(8,128)(2,1)S(1)} %get-tuple-element.9.ret, f32[1024,768]{1,0:T(8,128)S(1)} %get-tuple-element.10.dm_in, f32[8,128]{1,0:T(8,128)S(1)} %get-tuple-element.11.loss_in), custom_call_target="tpu_custom_call" | custom-call | tf_op jit(solution)/shard_map/collect/pallas_call | solution.py:279
Async XLA Ops:
  0.6 89.7 %copy-start = (s32[1,8]{1,0:T(1,128)S(1)}, s32[1,8]{1,0:T(1,128)}, u32[]{:S(2)}) copy-start(s32[1,8]{1,0:T(1,128)} %picks.3) | copy-start | bytes 100

commit v5 on v4

--- a/solution.py
+++ b/solution.py
@@ -31,11 +31,11 @@
 
 def exchange(
     picks, table, mentions, gold, ret, dm, loss,
-    part_a, part_b, part_c, part_d, ment_v, gold_v, send, cand, scores, dscore, gsend, lsend, lbuf,
+    part_a, part_b, part_c, part_d, part_e, part_f, part_g, part_h, ment_v, gold_v, send, cand, scores, dscore, gsend, lsend, lbuf,
     local_sem, fsend, frecv, bsend, brecv, lsend_sem, lrecv_sem,
 ):
     me = lax.axis_index("ent")
-    parts = (part_a, part_b, part_c, part_d)
+    parts = (part_a, part_b, part_c, part_d, part_e, part_f, part_g, part_h)
     depth = BLK // len(parts)
     loads = [
         pltpu.make_async_copy(table.at[:, pl.ds(q * depth, depth)], part, local_sem.at[q])
@@ -253,7 +253,7 @@
         in_specs=[pl.BlockSpec(memory_space=pltpu.SMEM), anywhere, anywhere, anywhere],
         out_specs=(vmem, vmem, vmem),
         scratch_shapes=[
-            *(pltpu.VMEM((BPD, BLK // 4, D), jnp.bfloat16) for _ in range(4)),
+            *(pltpu.VMEM((BPD, BLK // 8, D), jnp.bfloat16) for _ in range(8)),
             pltpu.VMEM((MEN, D), jnp.bfloat16),
             pltpu.VMEM((8, 128), jnp.int32),
             pltpu.VMEM((STEPS, BLK, D), jnp.bfloat16),
@@ -263,7 +263,7 @@
             pltpu.VMEM((STEPS, BLK, D), WIRE),
             pltpu.VMEM((4, 8, 128), jnp.float32),
             pltpu.VMEM((4, 4, 8, 128), jnp.float32),
-            pltpu.SemaphoreType.DMA((6,)),
+            pltpu.SemaphoreType.DMA((10,)),
             pltpu.SemaphoreType.DMA((STEPS,)),
             pltpu.SemaphoreType.DMA((STEPS,)),
             pltpu.SemaphoreType.DMA((1,)),

time: 97.3 us -> 97.3 us (level)
  no operation moved by 1% of the time
where the time goes in v5:
time: 97.3 us; the launch traced here: 97.2 us
  Pallas kernels  96.6 us (99%)
    pallas_call x1, Pallas kernels, on_device(): pl.pallas_call(exchange, out_shape=(pltpu.VMEM((ROUNDS, BLK, D), WIRE), p...  89.7 us
    pallas_call x1, Pallas kernels, on_device(): pl.pallas_call(collect, out_shape=(jax.ShapeDtypeStruct((BPD, BLK, D), jn...  6.83 us

profile of v5, /device:TPU:1, one launch (start us, length us, event | category | flops | bytes accessed | tf_op | source)
XLA Modules:
  0.0 97.2 jit_solution(17176812674300523439)
XLA Ops:
  0.6 0.0 copy-start
  0.6 89.7 %exchange.1 = (bf16[8,256,768]{2,1,0:T(8,128)(2,1)S(1)}, f32[1024,768]{1,0:T(8,128)S(1)}, f32[8,128]{1,0:T(8,128)S(1)}) custom-call(s32[1,8]{1,0:T(1,128)} %picks.3, bf16[16,256,768]{2,1,0:T(8,128)(2,1)} %bitcast.4, bf16[1024,768]{1,0:T(8,128)(2,1)} %mentions.1, s32[8,128]{1,0:T(8,128)} %bitcast.5), custom_call_target="tpu_custom_call" | custom-call | tf_op jit(solution)/shard_map/exchange/pallas_call | solution.py:246
  90.4 0.0 copy-done
  90.4 6.8 %collect.1 = (f32[16,256,768]{2,1,0:T(8,128)}, f32[1024,768]{1,0:T(8,128)}, f32[1,1]{1,0:T(1,128)}) custom-call(s32[1,8]{1,0:T(1,128)S(1)} %copy-done, bf16[8,256,768]{2,1,0:T(8,128)(2,1)S(1)} %get-tuple-element.9.ret, f32[1024,768]{1,0:T(8,128)S(1)} %get-tuple-element.10.dm_in, f32[8,128]{1,0:T(8,128)S(1)} %get-tuple-element.11.loss_in), custom_call_target="tpu_custom_call" | custom-call | tf_op jit(solution)/shard_map/collect/pallas_call | solution.py:279
Async XLA Ops:
  0.6 89.8 %copy-start = (s32[1,8]{1,0:T(1,128)S(1)}, s32[1,8]{1,0:T(1,128)}, u32[]{:S(2)}) copy-start(s32[1,8]{1,0:T(1,128)} %picks.3) | copy-start | bytes 100
